TPU v7x, 256 devices: a whole 4x4x8 slice. The times are simulated.
256 devices in a mesh: snp: 32 (over y, z), ind: 8 (over x, core).
Axes of the slice: x: 4, y: 4, z: 8, core: 2. Of those that a mesh axis runs over, the one named last changes fastest.
Arguments:
- beta_hat: float32 [64, 32768], P('ind', 'snp'), may hold values from -8 to 8
- ld_band: float32 [32768, 1024], P('snp'), as said below
- band_start: int32 [256], P('snp'), may hold values from -480 to 32224, as said below
- heritability: float32 [64], P('ind'), may hold values from 0.2 to 0.6
- genotypes: bfloat16 [8192, 32768], P('ind', 'snp'), may hold values from 0 to 2, as said below
Outputs:
- weights: float32 [64, 32768], P('ind', 'snp')
- scores: float32 [64, 8192], P(None, ('ind', 'snp'))
Inputs may be any that keep to these rules, and one draw needn't show every extreme that they name: ld_band is a symmetric matrix R in band form: entry k of row i is R[i, band_start[i // 128] + k]; R[i, i] = 1; R[i, j] = 0 when |i - j| > 416 or j lies outside the SNPs; the off-diagonal magnitudes of a row sum to 2.5 at most. `band_start`: block b's window starts at 128 * b - 416 - k with k from 0 to 64; the first block has k = 64 and the last block k = 0. `genotypes`: dosages are 0, 1 or 2.
All inputs are finite; a program needn't handle non-finite values.
Results may differ from a plain program's by a relative error of at most 0.0021.
Values may be sent and summed in bfloat16 or wider, within the bound.
A program may use at most 64 MiB of HBM per device.

v0:
```python
import jax
import jax.numpy as jnp
from jax import lax
from jax.sharding import PartitionSpec as P

BLK = 128
ITERS = 2
M_GENOME = 1100000
N_GWAS = 1000000


def padded_2(block, sides, width):
    for axis, dim in sides:
        count = lax.axis_size(axis)
        forward = [(i, i + 1) for i in range(count - 1)]
        backward = [(target, source) for source, target in forward]
        low = lax.ppermute(
            lax.slice_in_dim(block, block.shape[dim] - width, None, axis=dim), axis, forward
        )
        high = lax.ppermute(lax.slice_in_dim(block, 0, width, axis=dim), axis, backward)
        block = jnp.concatenate([low, block, high], axis=dim)
    return block


def apply_operator(vector, ld_band, band_start, ridge_shift):
    band_cols = ld_band.shape[1]
    halo_cols = band_cols - BLK
    padded = padded_2(vector, (("snp", 1),), halo_cols)
    local_rows = vector.shape[1]
    offsets = band_start - lax.axis_index("snp") * local_rows + halo_cols
    windows = jax.vmap(lambda row_begin: lax.dynamic_slice_in_dim(padded, row_begin, band_cols, 1))(
        offsets
    )
    blocks = ld_band.reshape(band_start.shape[0], BLK, band_cols)
    product = jnp.einsum("btk,brk->tbr", windows, blocks, precision=lax.Precision.HIGHEST)
    return product.reshape(vector.shape) + ridge_shift[:, None] * vector


def norm_sum(residual):
    return lax.psum(jnp.sum(residual * residual, axis=1), "snp")


def local(beta_hat, ld_band, band_start, heritability, genotypes):
    ridge_shift = M_GENOME / N_GWAS / heritability
    weights = jnp.zeros_like(beta_hat)
    residual = beta_hat
    direction = beta_hat
    norm_now = norm_sum(residual)
    for turn_index in range(ITERS):
        product = apply_operator(direction, ld_band, band_start, ridge_shift)
        curved = lax.psum(jnp.sum(direction * product, axis=1), "snp")
        step_size = norm_now / curved
        weights = weights + step_size[:, None] * direction
        residual = residual - step_size[:, None] * product
        if turn_index + 1 < ITERS:
            norm_next = norm_sum(residual)
            direction = residual + (norm_next / norm_now)[:, None] * direction
            norm_now = norm_next
    rounded = weights.astype(jnp.bfloat16)
    partial_scores = lax.dot_general(
        lax.all_gather(rounded, "ind", axis=0, tiled=True),
        genotypes,
        (((1,), (1,)), ((), ())),
        preferred_element_type=jnp.float32,
    )
    complete = lax.psum(partial_scores, "snp")
    count = complete.shape[1] * lax.axis_size("ind")
    summed = lax.psum(jnp.sum(complete, axis=1), "ind")
    average = summed / count
    centred = complete - average[:, None]
    variance = lax.psum(jnp.sum(centred * centred, axis=1), "ind") / count
    share_cols = complete.shape[1] // lax.axis_size("snp")
    own_part = lax.dynamic_slice_in_dim(centred, lax.axis_index("snp") * share_cols, share_cols, 1)
    scores = own_part * lax.rsqrt(variance + 1e-05)[:, None]
    return (weights, scores)


def solution(mesh):
    placed = (P("ind", "snp"), P("snp", None), P("snp"), P("ind"), P("ind", "snp"))
    return jax.shard_map(
        local,
        mesh=mesh,
        in_specs=placed,
        out_specs=(P("ind", "snp"), P(None, ("ind", "snp"))),
        check_vma=False,
    )
```

profile of v0, /device:TPU:1, one launch (start us, length us, event | category | flops | bytes accessed | tf_op | source)
XLA Modules:
  0.0 465.0 jit_solution(3514487914134571717)
XLA Ops:
  7.2 0.9 fusion.7
  8.1 4.4 collective-permute-start
  12.5 1.3 collective-permute-start.1
  15.2 2.2 collective-permute-done.1
  17.3 0.8 pad_maximum_fusion
  18.1 10.5 %while.2 = (s32[]{:T(128)}, f32[8,2816]{1,0:T(8,128)S(1)}, s32[8,2]{0,1:T(2,128)S(1)}, f32[8,8,1024]{2,1,0:T(8,128)S(1)}, s32[]{:T(128)}) while((s32[]{:T(128)}, f32[8,2816]{1,0:T(8,128)S(1)}, s32[8,2]{0,1:T(2,128)S(1)}, f32[8,8,1024]{2,1,0:T(8,128)S(1)}, s32[]{:T(128)}) %tuple.38), condition=%wide.while_cond, body=%wide.while_body.sunk | while | flops 2 | bytes 65633 | solution.py:31
  18.7 0.7 bitcast_dynamic-update-slice_fusion.4
  20.0 0.7 bitcast_dynamic-update-slice_fusion.4
  21.3 0.7 bitcast_dynamic-update-slice_fusion.4
  22.7 0.7 bitcast_dynamic-update-slice_fusion.4
  24.0 0.7 bitcast_dynamic-update-slice_fusion.4
  25.3 0.7 bitcast_dynamic-update-slice_fusion.4
  26.6 0.7 bitcast_dynamic-update-slice_fusion.4
  27.9 0.7 bitcast_dynamic-update-slice_fusion.4
  28.6 5.4 %multiply_reduce_fusion.2 = (f32[8]{0:T(128)S(1)}, f32[8]{0:T(128)S(1)}, f32[8,1024]{1,0:T(8,128)S(1)}) fusion(f32[8,1024]{1,0:T(8,128)} %param.5, f32[8]{0:T(128)S(1)} %broadcast_divide_fusion, f32[8,8,1024]{2,1,0:T(8,128)S(1)} %get-tuple-element.9, f32[8,128,1024]{2,1,0:T(8,128)} %bitcast.39), kind=kOutput, calls=%fused_computation.19 | convolution fusion | flops 100712432 | bytes 4522080 | tf_op jit(solution)/shard_map/btk,brk->tbr/dot_general | solution.py:35
  34.1 62.4 %all-reduce.1 = (f32[8]{0:T(128)S(1)}, f32[8]{0:T(128)S(1)}) all-reduce(f32[8]{0:T(128)S(1)} %get-tuple-element.21, f32[8]{0:T(128)S(1)} %get-tuple-element.20), channel_id=1, replica_groups=mesh['snp'=32,'ind'=8] {'snp'}, use_global_device_ids=true, to_apply=%region_1.0 | all-reduce | flops 16 | bytes 128 | tf_op jit(solution)/shard_map/psum | solution.py:40
  96.6 55.7 %psum.51 = f32[8]{0:T(128)S(1)} all-reduce(f32[8]{0:T(128)S(1)} %multiply_reduce_fusion.1), channel_id=1, replica_groups=mesh['snp'=32,'ind'=8] {'snp'}, use_global_device_ids=true, to_apply=%region_5.0 | all-reduce | flops 8 | bytes 64 | tf_op jit(solution)/shard_map/psum | solution.py:40
  152.5 3.6 collective-permute-start.2
  156.0 1.3 collective-permute-start.3
  157.3 3.6 collective-permute-done.3
  161.0 10.5 %while.3 = (s32[]{:T(128)}, f32[8,2816]{1,0:T(8,128)S(1)}, s32[8,2]{0,1:T(2,128)S(1)}, f32[8,8,1024]{2,1,0:T(8,128)S(1)}, s32[]{:T(128)}) while((s32[]{:T(128)}, f32[8,2816]{1,0:T(8,128)S(1)}, s32[8,2]{0,1:T(2,128)S(1)}, f32[8,8,1024]{2,1,0:T(8,128)S(1)}, s32[]{:T(128)}) %tuple.46), condition=%wide.while_cond.1, body=%wide.while_body.1.sunk | while | flops 2 | bytes 65633 | solution.py:31
  161.6 0.7 bitcast_dynamic-update-slice_fusion.5
  162.9 0.7 bitcast_dynamic-update-slice_fusion.5
  171.5 5.4 %fusion.3 = f32[8]{0:T(128)S(1)} fusion(f32[8,1024]{1,0:T(8,128)S(1)} %multiply_add_fusion.1, f32[8,8,1024]{2,1,0:T(8,128)S(1)} %get-tuple-element.17, f32[8,128,1024]{2,1,0:T(8,128)} %bitcast.40, f32[8]{0:T(128)S(1)} %broadcast_divide_fusion), kind=kOutput, calls=%fused_computation.9 | convolution fusion | flops 100696056 | bytes 4489280 | tf_op jit(solution)/shard_map/btk,brk->tbr/dot_general | solution.py:35
  176.9 55.7 %psum.52 = f32[8]{0:T(128)S(1)} all-reduce(f32[8]{0:T(128)S(1)} %fusion.3), channel_id=1, replica_groups=mesh['snp'=32,'ind'=8] {'snp'}, use_global_device_ids=true, to_apply=%region_7.0 | all-reduce | flops 8 | bytes 64 | tf_op jit(solution)/shard_map/psum | solution.py:51
  233.3 57.2 %all_gather.3 = bf16[64,1024]{1,0:T(8,128)(2,1)S(1)} all-gather(bf16[8,1024]{1,0:T(8,128)(2,1)S(1)} %get-tuple-element.42), channel_id=1, replica_groups=mesh['snp'=32,'ind'=8] {'ind'}, dimensions={0}, use_global_device_ids=true | all-gather | bytes 147456 | tf_op jit(solution)/shard_map/all_gather | solution.py:61
  290.5 1.5 fusion.8
  292.0 133.9 %all-reduce.4.cloned.1.call-done = f32[64,1024]{1,0:T(8,128)} async-done(((f32[64,1024]{1,0:T(8,128)}), f32[64,1024]{1,0:T(8,128)}) %all-reduce.4.cloned.1.call-update) | async-done | bytes 262160 | tf_op jit(solution)/shard_map/psum | solution.py:66
  425.9 1.1 reduce_sum.58
  426.9 16.9 %psum.54 = f32[64]{0:T(128)S(1)} all-reduce(f32[64]{0:T(128)S(1)} %reduce_sum.58), channel_id=1, replica_groups=mesh['snp'=32,'ind'=8] {'ind'}, use_global_device_ids=true, to_apply=%region_10.0 | all-reduce | flops 64 | bytes 512 | tf_op jit(solution)/shard_map/psum | solution.py:68
  443.8 1.1 multiply_reduce_fusion
  445.0 12.4 %psum.55 = f32[64]{0:T(128)S(1)} all-reduce(f32[64]{0:T(128)S(1)} %get-tuple-element.40), channel_id=1, replica_groups=mesh['snp'=32,'ind'=8] {'ind'}, use_global_device_ids=true, to_apply=%region_12.0 | all-reduce | flops 64 | bytes 512 | tf_op jit(solution)/shard_map/psum | solution.py:71
  (63 shorter events, 17.0 us)
Async XLA Ops:
  7.2 283.4 %copy-start = (bf16[1024,1024]{1,0:T(8,128)(2,1)S(1)}, bf16[1024,1024]{1,0:T(8,128)(2,1)}, u32[]{:S(2)}) copy-start(bf16[1024,1024]{1,0:T(8,128)(2,1)} %param.9) | copy-start | bytes 6291460
  7.2 89.3 %copy-start.1 = (f32[8,1024]{1,0:T(8,128)S(1)}, f32[8,1024]{1,0:T(8,128)}, u32[]{:S(2)}) copy-start(f32[8,1024]{1,0:T(8,128)} %param.5) | copy-start | bytes 98308
  7.2 418.7 %all-reduce.4.cloned.1.call-start = ((), (), s32[]{:S(2)}) async-start(), calls=%async_computation | async-start | bytes 524288 | tf_op jit(solution)/shard_map/psum | solution.py:66
  8.1 7.0 %collective-permute-start = (f32[8,896]{1,0:T(8,128)S(1)}, f32[8,896]{1,0:T(8,128)S(1)}, u32[]{:S(2)}, u32[]{:S(2)}) collective-permute-start(f32[8,896]{1,0:T(8,128)S(1)} %get-tuple-element.46), channel_id=1, source_target_pairs={{0,8},{8,16},{16,24},{24,32},{32,40},{40,48},{48,56},{56,64},{64,7... | collective-permute-start | bytes 86024 | tf_op jit(solution)/shard_map/ppermute | solution.py:17
  12.5 4.8 %collective-permute-start.1 = (f32[8,896]{1,0:T(8,128)S(1)}, f32[8,896]{1,0:T(8,128)S(1)}, u32[]{:S(2)}, u32[]{:S(2)}) collective-permute-start(f32[8,896]{1,0:T(8,128)S(1)} %get-tuple-element.47), channel_id=1, source_target_pairs={{8,0},{16,8},{24,16},{32,24},{40,32},{48,40},{56,48},{64,56},{72,6... | collective-permute-start | bytes 86024 | tf_op jit(solution)/shard_map/ppermute | solution.py:20
  152.5 4.9 %collective-permute-start.2 = (f32[8,896]{1,0:T(8,128)S(1)}, f32[8,896]{1,0:T(8,128)S(1)}, u32[]{:S(2)}, u32[]{:S(2)}) collective-permute-start(f32[8,896]{1,0:T(8,128)S(1)} %get-tuple-element.44), channel_id=1, source_target_pairs={{0,8},{8,16},{16,24},{24,32},{32,40},{40,48},{48,56},{56,64},{64,7... | collective-permute-start | bytes 86024 | tf_op jit(solution)/shard_map/ppermute | solution.py:17
  156.0 4.9 %collective-permute-start.3 = (f32[8,896]{1,0:T(8,128)S(1)}, f32[8,896]{1,0:T(8,128)S(1)}, u32[]{:S(2)}, u32[]{:S(2)}) collective-permute-start(f32[8,896]{1,0:T(8,128)S(1)} %get-tuple-element.45), channel_id=1, source_target_pairs={{8,0},{16,8},{24,16},{32,24},{40,32},{48,40},{56,48},{64,56},{72,6... | collective-permute-start | bytes 86024 | tf_op jit(solution)/shard_map/ppermute | solution.py:20
Sparse Core Ops, SparseCore 0:
  292.1 133.6 all-reduce.3
where the time goes:
time: 466 us; the launch traced here: 465 us
  blocking collectives  260 us (56%)
  waiting for transfers between devices  140 us (30%)
  local copies, waits for them, and re-layouts  22.7 us (5%)
  between operations  14.1 us (3%)
  matrix products  12.3 us (3%)
  starting transfers between devices  10.5 us (2%)
  other arithmetic  5.4 us (1%)
    psum x1, waiting for transfers between devices, local(): complete = lax.psum(partial_scores, 'snp')  134 us
    psum x2, blocking collectives, norm_sum(): return lax.psum(jnp.sum(residual * residual, axis=1), 'snp')  118 us
    all_gather x1, blocking collectives, local(): lax.all_gather(rounded, 'ind', axis=0, tiled=True)  57.2 us
    psum x1, blocking collectives, local(): curved = lax.psum(jnp.sum(direction * product, axis=1), 'snp')  55.7 us
    gather x48, local copies, waits for them, and re-layouts  21 us
    psum x1, blocking collectives, local(): summed = lax.psum(jnp.sum(complete, axis=1), 'ind')  16.9 us
    psum x1, blocking collectives, local(): variance = lax.psum(jnp.sum(centred * centred, axis=1), 'ind') / count  12.4 us
    dot_general x2, matrix products, apply_operator(): jnp.einsum('btk,brk->tbr', windows, blocks, precision=lax.Precision.HIGHEST)  10.8 us
  transfers between devices with their start and end apart: 5, of which 3 were waited for; matrix products, arithmetic and copies ran while one was open for 0% of the time, Pallas kernels for 0%

commit v1 on v0

--- a/solution.py
+++ b/solution.py
@@ -63,7 +63,8 @@
         (((1,), (1,)), ((), ())),
         preferred_element_type=jnp.float32,
     )
-    complete = lax.psum(partial_scores, "snp")
+    terms = lax.all_gather(partial_scores, "snp")
+    complete = jnp.sum(terms, axis=0)
     count = complete.shape[1] * lax.axis_size("ind")
     summed = lax.psum(jnp.sum(complete, axis=1), "ind")
     average = summed / count

time: 466 us -> 428 us (0.918)
  waiting for transfers between devices: 140 us -> 98.1 us
  other arithmetic: 5.4 us -> 11.2 us
    psum x1 -> x0, waiting for transfers between devices: 134 us -> none  [local(): complete = lax.psum(partial_scores, 'snp')]
    all_gather x0 -> x1, waiting for transfers between devices: none -> 92.3 us  [local(): terms = lax.all_gather(partial_scores, 'snp')]
where the time goes in v1:
time: 428 us; the launch traced here: 427 us
  blocking collectives  258 us (60%)
  waiting for transfers between devices  98.1 us (23%)
  local copies, waits for them, and re-layouts  22.7 us (5%)
  between operations  14.1 us (3%)
  matrix products  12.3 us (3%)
  other arithmetic  11.2 us (3%)
  starting transfers between devices  10.5 us (2%)
    psum x2, blocking collectives, norm_sum(): return lax.psum(jnp.sum(residual * residual, axis=1), 'snp')  118 us
    all_gather x1, waiting for transfers between devices, local(): terms = lax.all_gather(partial_scores, 'snp')  92.3 us
    all_gather x1, blocking collectives, local(): lax.all_gather(rounded, 'ind', axis=0, tiled=True)  57.2 us
    psum x1, blocking collectives, local(): curved = lax.psum(jnp.sum(direction * product, axis=1), 'snp')  55.7 us
    gather x48, local copies, waits for them, and re-layouts  21 us
    psum x1, blocking collectives, local(): variance = lax.psum(jnp.sum(centred * centred, axis=1), 'ind') / count  14.1 us
    psum x1, blocking collectives, local(): summed = lax.psum(jnp.sum(complete, axis=1), 'ind')  12.9 us
    dot_general x2, matrix products, apply_operator(): jnp.einsum('btk,brk->tbr', windows, blocks, precision=lax.Precision.HIGHEST)  10.8 us
  transfers between devices with their start and end apart: 5, of which 3 were waited for; matrix products, arithmetic and copies ran while one was open for 0% of the time, Pallas kernels for 0%

profile of v1, /device:TPU:1, one launch (start us, length us, event | category | flops | bytes accessed | tf_op | source)
XLA Modules:
  0.0 427.0 jit_solution(4329994094951306491)
XLA Ops:
  7.2 0.9 fusion.7
  8.1 4.4 %collective-permute-start = (f32[8,896]{1,0:T(8,128)S(1)}, f32[8,896]{1,0:T(8,128)S(1)}, u32[]{:S(2)}, u32[]{:S(2)}) collective-permute-start(f32[8,896]{1,0:T(8,128)S(1)} %get-tuple-element.48), channel_id=1, source_target_pairs={{0,8},{8,16},{16,24},{24,32},{32,40},{40,48},{48,56},{56,64},{64,7... | collective-permute-start | bytes 86024 | tf_op jit(solution)/shard_map/ppermute | solution.py:17
  12.5 1.3 collective-permute-start.1
  15.2 2.2 collective-permute-done.1
  17.3 0.8 pad_maximum_fusion
  18.1 10.5 %while.2 = (s32[]{:T(128)}, f32[8,2816]{1,0:T(8,128)S(1)}, s32[8,2]{0,1:T(2,128)S(1)}, f32[8,8,1024]{2,1,0:T(8,128)S(1)}, s32[]{:T(128)}) while((s32[]{:T(128)}, f32[8,2816]{1,0:T(8,128)S(1)}, s32[8,2]{0,1:T(2,128)S(1)}, f32[8,8,1024]{2,1,0:T(8,128)S(1)}, s32[]{:T(128)}) %tuple.39), condition=%wide.while_cond, body=%wide.while_body.sunk | while | flops 2 | bytes 65641 | solution.py:31
  18.7 0.7 bitcast_dynamic-update-slice_fusion.4
  20.0 0.7 bitcast_dynamic-update-slice_fusion.4
  21.3 0.7 bitcast_dynamic-update-slice_fusion.4
  22.7 0.7 bitcast_dynamic-update-slice_fusion.4
  24.0 0.7 bitcast_dynamic-update-slice_fusion.4
  25.3 0.7 bitcast_dynamic-update-slice_fusion.4
  26.6 0.7 bitcast_dynamic-update-slice_fusion.4
  27.9 0.7 bitcast_dynamic-update-slice_fusion.4
  28.6 5.4 %multiply_reduce_fusion.2 = (f32[8]{0:T(128)S(1)}, f32[8]{0:T(128)S(1)}, f32[8,1024]{1,0:T(8,128)S(1)}) fusion(f32[8,1024]{1,0:T(8,128)} %param.5, f32[8]{0:T(128)S(1)} %broadcast_divide_fusion, f32[8,8,1024]{2,1,0:T(8,128)S(1)} %get-tuple-element.9, f32[8,128,1024]{2,1,0:T(8,128)} %bitcast.41), kind=kOutput, calls=%fused_computation.19 | convolution fusion | flops 100712432 | bytes 4522080 | tf_op jit(solution)/shard_map/btk,brk->tbr/dot_general | solution.py:35
  34.1 62.4 %all-reduce.1 = (f32[8]{0:T(128)S(1)}, f32[8]{0:T(128)S(1)}) all-reduce(f32[8]{0:T(128)S(1)} %get-tuple-element.23, f32[8]{0:T(128)S(1)} %get-tuple-element.22), channel_id=1, replica_groups=mesh['snp'=32,'ind'=8] {'snp'}, use_global_device_ids=true, to_apply=%region_1.0 | all-reduce | flops 16 | bytes 128 | tf_op jit(solution)/shard_map/psum | solution.py:40
  96.6 55.7 %psum.44 = f32[8]{0:T(128)S(1)} all-reduce(f32[8]{0:T(128)S(1)} %multiply_reduce_fusion.1), channel_id=1, replica_groups=mesh['snp'=32,'ind'=8] {'snp'}, use_global_device_ids=true, to_apply=%region_5.0 | all-reduce | flops 8 | bytes 64 | tf_op jit(solution)/shard_map/psum | solution.py:40
  152.5 3.6 collective-permute-start.2
  156.0 1.3 collective-permute-start.3
  157.3 3.6 collective-permute-done.3
  161.0 10.5 %while.3 = (s32[]{:T(128)}, f32[8,2816]{1,0:T(8,128)S(1)}, s32[8,2]{0,1:T(2,128)S(1)}, f32[8,8,1024]{2,1,0:T(8,128)S(1)}, s32[]{:T(128)}) while((s32[]{:T(128)}, f32[8,2816]{1,0:T(8,128)S(1)}, s32[8,2]{0,1:T(2,128)S(1)}, f32[8,8,1024]{2,1,0:T(8,128)S(1)}, s32[]{:T(128)}) %tuple.47), condition=%wide.while_cond.1, body=%wide.while_body.1.sunk | while | flops 2 | bytes 65641 | solution.py:31
  161.6 0.7 bitcast_dynamic-update-slice_fusion.5
  162.9 0.7 bitcast_dynamic-update-slice_fusion.5
  171.5 5.4 %fusion.3 = f32[8]{0:T(128)S(1)} fusion(f32[8,1024]{1,0:T(8,128)S(1)} %multiply_add_fusion.1, f32[8,8,1024]{2,1,0:T(8,128)S(1)} %get-tuple-element.17, f32[8,128,1024]{2,1,0:T(8,128)} %bitcast.42, f32[8]{0:T(128)S(1)} %broadcast_divide_fusion), kind=kOutput, calls=%fused_computation.9 | convolution fusion | flops 100696056 | bytes 4489280 | tf_op jit(solution)/shard_map/btk,brk->tbr/dot_general | solution.py:35
  176.9 55.7 %psum.45 = f32[8]{0:T(128)S(1)} all-reduce(f32[8]{0:T(128)S(1)} %fusion.3), channel_id=1, replica_groups=mesh['snp'=32,'ind'=8] {'snp'}, use_global_device_ids=true, to_apply=%region_7.0 | all-reduce | flops 8 | bytes 64 | tf_op jit(solution)/shard_map/psum | solution.py:51
  233.3 57.2 %all_gather.9 = bf16[64,1024]{1,0:T(8,128)(2,1)S(1)} all-gather(bf16[8,1024]{1,0:T(8,128)(2,1)S(1)} %get-tuple-element.44), channel_id=1, replica_groups=mesh['snp'=32,'ind'=8] {'ind'}, dimensions={0}, use_global_device_ids=true | all-gather | bytes 147456 | tf_op jit(solution)/shard_map/all_gather | solution.py:61
  290.5 1.5 fusion.8
  292.0 92.3 %all-gather.3.cloned.1.call-done = f32[2048,1024]{1,0:T(8,128)} async-done(((f32[64,1024]{1,0:T(8,128)}), f32[2048,1024]{1,0:T(8,128)}) %all-gather.3.cloned.1.call-update) | async-done | bytes 8388624 | tf_op jit(solution)/shard_map/all_gather | solution.py:66
  384.3 3.8 reduce.1
  388.3 12.9 %psum.46 = f32[64]{0:T(128)S(1)} all-reduce(f32[64]{0:T(128)S(1)} %reduce_sum.68), channel_id=1, replica_groups=mesh['snp'=32,'ind'=8] {'ind'}, use_global_device_ids=true, to_apply=%region_10.0 | all-reduce | flops 64 | bytes 512 | tf_op jit(solution)/shard_map/psum | solution.py:69
  401.1 4.0 reduce_sum.67
  405.3 14.1 %psum.47 = f32[64]{0:T(128)S(1)} all-reduce(f32[64]{0:T(128)S(1)} %get-tuple-element.42), channel_id=1, replica_groups=mesh['snp'=32,'ind'=8] {'ind'}, use_global_device_ids=true, to_apply=%region_12.0 | all-reduce | flops 64 | bytes 512 | tf_op jit(solution)/shard_map/psum | solution.py:72
  (66 shorter events, 17.3 us)
Async XLA Ops:
  7.2 283.4 %copy-start = (bf16[1024,1024]{1,0:T(8,128)(2,1)S(1)}, bf16[1024,1024]{1,0:T(8,128)(2,1)}, u32[]{:S(2)}) copy-start(bf16[1024,1024]{1,0:T(8,128)(2,1)} %param.9) | copy-start | bytes 6291460
  7.2 89.3 %copy-start.1 = (f32[8,1024]{1,0:T(8,128)S(1)}, f32[8,1024]{1,0:T(8,128)}, u32[]{:S(2)}) copy-start(f32[8,1024]{1,0:T(8,128)} %param.5) | copy-start | bytes 98308
  7.2 377.1 %all-gather.3.cloned.1.call-start = ((), (), s32[]{:S(2)}) async-start(), calls=%async_computation | async-start | bytes 8650752 | tf_op jit(solution)/shard_map/all_gather | solution.py:66
  8.1 7.0 %collective-permute-start = (f32[8,896]{1,0:T(8,128)S(1)}, f32[8,896]{1,0:T(8,128)S(1)}, u32[]{:S(2)}, u32[]{:S(2)}) collective-permute-start(f32[8,896]{1,0:T(8,128)S(1)} %get-tuple-element.48), channel_id=1, source_target_pairs={{0,8},{8,16},{16,24},{24,32},{32,40},{40,48},{48,56},{56,64},{64,7... | collective-permute-start | bytes 86024 | tf_op jit(solution)/shard_map/ppermute | solution.py:17
  12.5 4.8 %collective-permute-start.1 = (f32[8,896]{1,0:T(8,128)S(1)}, f32[8,896]{1,0:T(8,128)S(1)}, u32[]{:S(2)}, u32[]{:S(2)}) collective-permute-start(f32[8,896]{1,0:T(8,128)S(1)} %get-tuple-element.49), channel_id=1, source_target_pairs={{8,0},{16,8},{24,16},{32,24},{40,32},{48,40},{56,48},{64,56},{72,6... | collective-permute-start | bytes 86024 | tf_op jit(solution)/shard_map/ppermute | solution.py:20
  152.5 4.9 %collective-permute-start.2 = (f32[8,896]{1,0:T(8,128)S(1)}, f32[8,896]{1,0:T(8,128)S(1)}, u32[]{:S(2)}, u32[]{:S(2)}) collective-permute-start(f32[8,896]{1,0:T(8,128)S(1)} %get-tuple-element.46), channel_id=1, source_target_pairs={{0,8},{8,16},{16,24},{24,32},{32,40},{40,48},{48,56},{56,64},{64,7... | collective-permute-start | bytes 86024 | tf_op jit(solution)/shard_map/ppermute | solution.py:17
  156.0 4.9 %collective-permute-start.3 = (f32[8,896]{1,0:T(8,128)S(1)}, f32[8,896]{1,0:T(8,128)S(1)}, u32[]{:S(2)}, u32[]{:S(2)}) collective-permute-start(f32[8,896]{1,0:T(8,128)S(1)} %get-tuple-element.47), channel_id=1, source_target_pairs={{8,0},{16,8},{24,16},{32,24},{40,32},{48,40},{56,48},{64,56},{72,6... | collective-permute-start | bytes 86024 | tf_op jit(solution)/shard_map/ppermute | solution.py:20
Sparse Core Ops, SparseCore 0:
  292.1 92.1 all-gather.2
